TPU v7x, 128 devices: a whole 4x4x4 slice. The times are simulated.
128 devices in a mesh: dp: 32 (over z, y, core), mp: 4 (over x).
Axes of the slice: x: 4, y: 4, z: 4, core: 2. Of those that a mesh axis runs over, the one named last changes fastest.
Arguments:
- patches: bfloat16 [49152, 128], P(('dp', 'mp')), may hold values from -6 to 6
- row_count: int32 [128], P(('dp', 'mp')), may hold values from 0 to 384, as said below
- target_group: int32 [49152], P(('dp', 'mp')), may hold values from 0 to 31, as said below
- target_offset: int32 [49152], P(('dp', 'mp')), may hold values from 0 to 639, as said below
- embed: bfloat16 [128, 6144], replicated, may hold values from -0.5 to 0.5
- norm_gain: bfloat16 [6144], replicated, may hold values from 0.099609375 to 1.8984375
- readout: bfloat16 [6144, 128], P('mp'), may hold values from -0.078125 to 0.078125
- target: bfloat16 [20480, 128], P('dp'), may hold values from -12 to 12
- master: float32 [6144, 6144], P('dp', 'mp'), may hold values from -6 to 6
- moment1: float32 [6144, 6144], P('dp', 'mp'), may hold values from -2 to 2
- moment2: float32 [6144, 6144], P('dp', 'mp'), may hold values from 0.0034722222 to 0.1388889
Outputs:
- prediction: float32 [20480, 128], P('dp')
- master_new: float32 [6144, 6144], P('dp', 'mp')
- moment1_new: float32 [6144, 6144], P('dp', 'mp')
- moment2_new: float32 [6144, 6144], P('dp', 'mp')
- weight_copy: bfloat16 [6144, 6144], P('dp', 'mp')
Inputs may be any that keep to these rules, and one draw needn't show every extreme that they name: Device i holds its live patch rows in its first row_count[i] slots; some device holds 384 of them in every draw. Over the live slots of all devices, each pair (target_group, target_offset) of the 20480 positions occurs exactly once; values in slots past row_count are arbitrary within the range. Call target_offset // 160 the block of a row. Each (batch, block) receives exactly 160 live rows; one device sends at most 3 live rows to one (batch, block), and every (batch, block) gets 3 rows from some device.
All inputs are finite; a program needn't handle non-finite values.
Results may differ from a plain program's by a relative error of at most 0.03.
Values may be sent and summed in bfloat16 or wider, within the bound.
A program may use at most 128 MiB of HBM per device.

v0:
```python
import jax
import jax.numpy as jnp
from jax import lax
from jax.sharding import PartitionSpec as P

gelu_const = 0.7978845608028654
beta_one = 0.9
beta_two = 0.95
learn_rate = 0.01
decay_rate = 0.1
adam_epsilon = 1e-08
step_count = 20


def gelu_tanh(value):
    inner = gelu_const * (value + 0.044715 * value * value * value)
    return 0.5 * value * (1.0 + jnp.tanh(inner))


def gelu_slope(value):
    tangent = jnp.tanh(gelu_const * (value + 0.044715 * value * value * value))
    return 0.5 * (1.0 + tangent) + 0.5 * value * (1.0 - tangent * tangent) * gelu_const * (
        1.0 + 3.0 * 0.044715 * value * value
    )


def shards(
    patches,
    row_count,
    target_group,
    target_offset,
    embed,
    norm_gain,
    readout,
    target,
    master,
    moment1,
    moment2,
):
    model_count = lax.axis_size("mp")
    batch_count = lax.axis_size("dp")
    devices_all = batch_count * model_count
    slot_total = patches.shape[0]
    capacity = slot_total // devices_all
    batch_rows = target.shape[0]
    block_rows = batch_rows // model_count
    width = embed.shape[1]
    patch_width = patches.shape[1]
    occupied = jnp.arange(slot_total, dtype=jnp.int32) < row_count[0]
    owner_index = jnp.where(
        occupied, target_group * model_count + target_offset // block_rows, devices_all
    )
    onehot = (owner_index[:, None] == jnp.arange(devices_all, dtype=jnp.int32)[None, :]).astype(
        jnp.int32
    )
    running = jnp.cumsum(onehot, axis=0)
    placing = jnp.sum(onehot * running, axis=1) - 1
    send_slot = jnp.where(occupied, owner_index * capacity + placing, devices_all * capacity)
    outgoing = (
        jnp.zeros((devices_all * capacity, patch_width), jnp.bfloat16)
        .at[send_slot]
        .set(patches, mode="drop")
    )
    slot_marks = (
        jnp.full((devices_all * capacity,), block_rows, jnp.int32)
        .at[send_slot]
        .set(target_offset % block_rows, mode="drop")
    )
    arrived, arrived_marks = (
        lax.all_to_all(outgoing, ("dp", "mp"), split_axis=0, concat_axis=0, tiled=True),
        lax.all_to_all(slot_marks, ("dp", "mp"), split_axis=0, concat_axis=0, tiled=True),
    )
    block_patches = (
        jnp.zeros((block_rows, patch_width), jnp.bfloat16)
        .at[arrived_marks]
        .set(arrived, mode="drop")
    )
    gain_wide = norm_gain.astype(jnp.float32)
    hidden = gelu_tanh(
        jnp.dot(
            lax.all_gather(block_patches, "mp", axis=0, tiled=True),
            embed,
            preferred_element_type=jnp.float32,
        )
    )
    normed = (
        hidden * lax.rsqrt(jnp.mean(hidden * hidden, axis=-1, keepdims=True) + 1e-05) * gain_wide
    ).astype(jnp.bfloat16)
    weight = master.astype(jnp.bfloat16)
    width_scale = 1.0 / width**0.5
    columns = normed
    preact = (
        jnp.dot(
            columns,
            lax.all_gather(weight, "dp", axis=0, tiled=True),
            preferred_element_type=jnp.float32,
        )
        * width_scale
    )
    activation = gelu_tanh(preact).astype(jnp.bfloat16)
    prediction = lax.psum(
        jnp.dot(activation, readout, preferred_element_type=jnp.float32).astype(jnp.bfloat16), "mp"
    ).astype(jnp.float32)
    errors = (prediction - target.astype(jnp.float32)).astype(jnp.bfloat16)
    backward = lax.dot_general(
        errors, readout, (((1,), (1,)), ((), ())), preferred_element_type=jnp.float32
    )
    delta_rows = (backward * gelu_slope(preact)).astype(jnp.bfloat16)
    columns = normed
    gradient = lax.psum_scatter(
        (
            lax.dot_general(
                columns, delta_rows, (((0,), (0,)), ((), ())), preferred_element_type=jnp.float32
            )
            * width_scale
        ).astype(jnp.bfloat16),
        "dp",
        scatter_dimension=0,
        tiled=True,
    ).astype(jnp.float32)
    moment1_new = beta_one * moment1 + (1.0 - beta_one) * gradient
    moment2_new = beta_two * moment2 + (1.0 - beta_two) * gradient * gradient
    first_fix = moment1_new / (1.0 - beta_one**step_count)
    second_fix = moment2_new / (1.0 - beta_two**step_count)
    master_new = master - learn_rate * (
        first_fix / (jnp.sqrt(second_fix) + adam_epsilon) + decay_rate * master
    )
    return (prediction, master_new, moment1_new, moment2_new, master_new.astype(jnp.bfloat16))


def solution(mesh):
    placed = (
        P(("dp", "mp"), None),
        P(("dp", "mp")),
        P(("dp", "mp")),
        P(("dp", "mp")),
        P(),
        P(),
        P("mp", None),
        P("dp", None),
        P("dp", "mp"),
        P("dp", "mp"),
        P("dp", "mp"),
    )
    return jax.shard_map(
        shards,
        mesh=mesh,
        in_specs=placed,
        out_specs=(P("dp", None), P("dp", "mp"), P("dp", "mp"), P("dp", "mp"), P("dp", "mp")),
        check_vma=False,
    )
```

profile of v0, /device:TPU:0, one launch (start us, length us, event | category | flops | bytes accessed | tf_op | source)
XLA Modules:
  0.0 316.7 jit_solution(15524870666545750787)
XLA Ops:
  7.2 0.0 copy-start
  7.2 0.0 copy-start.4
  7.2 0.0 all-gather.2.cloned.1.call-start
  7.2 2.3 convert_element_type.44
  9.5 0.0 all-gather.2.cloned.1.call-update
  10.2 0.7 add_select_fusion
  10.9 0.1 copy.18
  11.0 0.2 fusion.14
  11.3 0.1 broadcast_add_fusion
  11.3 0.2 fusion.16
  11.6 2.9 scatter_custom_fusion
  14.5 0.8 all_to_all.16
  15.3 11.1 %all-to-all-start = ((s32[128,3,1]{1,2,0:T(1,128)}), s32[128,3,1]{1,2,0:T(1,128)S(1)}, u32[]{:S(2)}, u32[]{:S(2)}) async-start(s32[128,3,1]{1,2,0:T(1,128)} %bitcast.5), calls=%async_computation | async-start | bytes 131072 | tf_op jit(solution)/shard_map/all_to_all | solution.py:71
  26.5 0.0 copy-done.4
  26.5 1.8 scatter_custom_fusion.1
  28.3 0.7 all_to_all.19
  29.0 6.7 %all-to-all-done = s32[128,3,1]{1,2,0:T(1,128)S(1)} async-done(((s32[128,3,1]{1,2,0:T(1,128)}), s32[128,3,1]{1,2,0:T(1,128)S(1)}, u32[]{:S(2)}, u32[]{:S(2)}) %all-to-all-start) | async-done | bytes 1568 | tf_op jit(solution)/shard_map/all_to_all | solution.py:71
  35.7 4.6 %all-to-all-start.1 = ((bf16[128,3,128]{2,1,0:T(4,128)(2,1)}), bf16[128,3,128]{2,1,0:T(4,128)(2,1)S(1)}, u32[]{:S(2)}, u32[]{:S(2)}) async-start(bf16[128,3,128]{2,1,0:T(4,128)(2,1)} %all_to_all.19), calls=%async_computation.1 | async-start | bytes 262144 | tf_op jit(solution)/shard_map/all_to_all | solution.py:70
  40.4 0.0 all-reduce.2.cloned.1.call-start
  40.4 0.5 broadcast.113
  40.9 0.8 reduce.5
  41.7 0.2 all_to_all.18
  42.0 7.9 %all-to-all-done.1 = bf16[128,3,128]{2,1,0:T(4,128)(2,1)S(1)} async-done(((bf16[128,3,128]{2,1,0:T(4,128)(2,1)}), bf16[128,3,128]{2,1,0:T(4,128)(2,1)S(1)}, u32[]{:S(2)}, u32[]{:S(2)}) %all-to-all-start.1) | async-done | bytes 98336 | tf_op jit(solution)/shard_map/all_to_all | solution.py:70
  49.8 0.1 reshape.88
  49.9 1.4 scatter_custom_fusion.2
  51.4 12.2 %all_gather.6 = bf16[640,128]{1,0:T(8,128)(2,1)S(1)} all-gather(bf16[160,128]{1,0:T(8,128)(2,1)S(1)} %scatter_custom_fusion.2), channel_id=1, replica_groups=mesh['dp'=32,'mp'=4] {'mp'}, dimensions={0}, use_global_device_ids=true | all-gather | bytes 204800 | tf_op jit(solution)/shard_map/all_gather | solution.py:81
  63.6 0.0 copy-done
  63.6 9.0 %multiply_reduce_fusion = (f32[640]{0:T(1024)S(1)}, f32[640,6144]{1,0:T(8,128)}) fusion(bf16[640,128]{1,0:T(8,128)(2,1)S(1)} %all_gather.6, bf16[128,6144]{1,0:T(8,128)(2,1)S(1)} %copy-done), kind=kOutput, calls=%fused_computation.10 | convolution fusion | flops 1045953920 | bytes 17467904 | tf_op jit(solution)/shard_map/dot_general | solution.py:80
  72.6 19.0 %all-gather.2.cloned.1.call-done = bf16[6144,1536]{1,0:T(8,128)(2,1)} async-done(((bf16[192,1536]{1,0:T(8,128)(2,1)}), bf16[6144,1536]{1,0:T(8,128)(2,1)}) %all-gather.2.cloned.1.call-update) | async-done | bytes 18874384 | tf_op jit(solution)/shard_map/all_gather | solution.py:95
  91.6 18.6 %fusion.40 = f32[640,1536]{1,0:T(8,128)S(1)} fusion(bf16[6144,1536]{1,0:T(8,128)(2,1)} %all-gather.2.cloned.1.call-done, f32[640,6144]{1,0:T(8,128)} %get-tuple-element.12, f32[6144]{0:T(1024)S(1)} %convert_element_type.42, f32[640]{0:T(1024)S(1)} %add_rsqrt_fusion), kind=kOutput, calls=%fused_computation.67 | convolution fusion | flops 12091392000 | bytes 38562304 | tf_op jit(solution)/shard_map/dot_general | solution.py:93
  110.2 0.0 copy-start.7
  110.2 2.0 copy-done.7
  112.2 0.0 copy-done.5
  112.2 2.2 fusion.13
  114.4 0.0 all-reduce.2.cloned.1.call-update
  114.4 0.3 reduce-scatter.2.cloned.1.call-start
  114.7 40.5 %all-reduce.2.cloned.1.call-done = bf16[640,128]{1,0:T(8,128)(2,1)} async-done(((bf16[640,128]{1,0:T(8,128)(2,1)}), bf16[640,128]{1,0:T(8,128)(2,1)}) %all-reduce.2.cloned.1.call-update) | async-done | bytes 163856 | tf_op jit(solution)/shard_map/psum | solution.py:101
  155.2 0.9 convert_element_type.47
  156.1 0.0 copy-done.6
  156.1 0.0 copy-start.3
  156.1 27.2 %multiply_convert_fusion = bf16[6144,1536]{1,0:T(8,128)(2,1)} fusion(f32[640,1536]{1,0:T(8,128)} %copy-done.7, bf16[1536,128]{1,0:T(8,128)(2,1)S(1)} %copy-done.5, f32[640,128]{1,0:T(8,128)S(1)} %convert_element_type.47, bf16[640,128]{1,0:T(8,128)(2,1)S(1)} %copy-done.6, f32[640,6144]{1,0:T(8,128)} %get-tuple-element.12, f32[6144]{0:T(1024)S(1)} %convert_element_type.42, ...), kind=kOutput, calls=%fused_computation.3 | convolution fusion | flops 12381831168 | bytes 39447040 | tf_op jit(solution)/shard_map/dot_general | solution.py:112
  183.4 0.0 copy-done.3
  183.4 0.0 reduce-scatter.2.cloned.1.call-update
  183.4 0.0 copy-start.1
  183.4 122.3 %reduce-scatter.2.cloned.1.call-done = bf16[192,1536]{1,0:T(8,128)(2,1)} async-done(((bf16[6144,1536]{1,0:T(8,128)(2,1)}), bf16[192,1536]{1,0:T(8,128)(2,1)}) %reduce-scatter.2.cloned.1.call-update) | async-done | bytes 589840 | tf_op jit(solution)/shard_map/reduce_scatter | solution.py:110
  305.7 0.0 copy-done.2
  305.7 4.4 %fusion.41 = (bf16[192,1536]{1,0:T(8,128)(2,1)}, f32[192,1536]{1,0:T(8,128)}, f32[192,1536]{1,0:T(8,128)}, f32[192,1536]{1,0:T(8,128)}) fusion(f32[192,1536]{1,0:T(8,128)S(1)} %copy-done.2, bf16[192,1536]{1,0:T(8,128)(2,1)} %reduce-scatter.2.cloned.1.call-done, f32[192,1536]{1,0:T(8,128)} %param.20, f32[192,1536]{1,0:T(8,128)} %param.21), kind=kLoop, calls=%fused_computation.68 | loop fusion | flops 5013504 | bytes 8257536 | tf_op jit(solution)/shard_map/convert_element_type | solution.py:128
  310.1 0.0 copy-done.1
  (10 shorter events, 0.1 us)
Async XLA Ops:
  7.2 56.4 %copy-start = (bf16[128,6144]{1,0:T(8,128)(2,1)S(1)}, bf16[128,6144]{1,0:T(8,128)(2,1)}, u32[]{:S(2)}) copy-start(bf16[128,6144]{1,0:T(8,128)(2,1)} %param.15) | copy-start | bytes 4718596
  7.2 19.3 %copy-start.4 = (bf16[6144]{0:T(1024)(128)(2,1)S(1)}, bf16[6144]{0:T(1024)(128)(2,1)}, u32[]{:S(2)}) copy-start(bf16[6144]{0:T(1024)(128)(2,1)} %param.16) | copy-start | bytes 36868
  7.2 84.4 %all-gather.2.cloned.1.call-start = ((), (), s32[]{:S(2)}) async-start(), calls=%async_computation.3 | async-start | bytes 19464192 | tf_op jit(solution)/shard_map/all_gather | solution.py:95
  15.3 20.4 %all-to-all-start = ((s32[128,3,1]{1,2,0:T(1,128)}), s32[128,3,1]{1,2,0:T(1,128)S(1)}, u32[]{:S(2)}, u32[]{:S(2)}) async-start(s32[128,3,1]{1,2,0:T(1,128)} %bitcast.5), calls=%async_computation | async-start | bytes 131072 | tf_op jit(solution)/shard_map/all_to_all | solution.py:71
  35.7 14.1 %all-to-all-start.1 = ((bf16[128,3,128]{2,1,0:T(4,128)(2,1)}), bf16[128,3,128]{2,1,0:T(4,128)(2,1)S(1)}, u32[]{:S(2)}, u32[]{:S(2)}) async-start(bf16[128,3,128]{2,1,0:T(4,128)(2,1)} %all_to_all.19), calls=%async_computation.1 | async-start | bytes 262144 | tf_op jit(solution)/shard_map/all_to_all | solution.py:70
  40.4 114.8 %all-reduce.2.cloned.1.call-start = ((), (), s32[]{:S(2)}) async-start(), calls=%async_computation.4 | async-start | bytes 327680 | tf_op jit(solution)/shard_map/psum | solution.py:101
  91.6 20.6 %copy-start.5 = (bf16[1536,128]{1,0:T(8,128)(2,1)S(1)}, bf16[1536,128]{1,0:T(8,128)(2,1)}, u32[]{:S(2)}) copy-start(bf16[1536,128]{1,0:T(8,128)(2,1)} %param.17) | copy-start | bytes 1179652
  110.2 2.0 copy-start.7
  112.2 43.9 %copy-start.6 = (bf16[640,128]{1,0:T(8,128)(2,1)S(1)}, bf16[640,128]{1,0:T(8,128)(2,1)}, u32[]{:S(2)}) copy-start(bf16[640,128]{1,0:T(8,128)(2,1)} %param.18) | copy-start | bytes 491524
  114.4 191.3 %reduce-scatter.2.cloned.1.call-start = ((), (), s32[]{:S(2)}) async-start(), calls=%async_computation.5 | async-start | bytes 19464192 | tf_op jit(solution)/shard_map/reduce_scatter | solution.py:110
  156.1 27.3 %copy-start.3 = (f32[640,128]{1,0:T(8,128)}, f32[640,128]{1,0:T(8,128)S(1)}, u32[]{:S(2)}) copy-start(f32[640,128]{1,0:T(8,128)S(1)} %convert_element_type.47) | copy-start | bytes 983044
  183.4 122.3 %copy-start.2 = (f32[192,1536]{1,0:T(8,128)S(1)}, f32[192,1536]{1,0:T(8,128)}, u32[]{:S(2)}) copy-start(f32[192,1536]{1,0:T(8,128)} %param.19) | copy-start | bytes 3538948
  183.4 126.7 %copy-start.1 = (bf16[128,6144]{1,0:T(8,128)(2,1)S(1)}, bf16[128,6144]{1,0:T(8,128)(2,1)}, u32[]{:S(2)}) copy-start(bf16[128,6144]{1,0:T(8,128)(2,1)} %param.15) | copy-start | bytes 4718596
Sparse Core Ops, SparseCore 0:
  10.9 80.6 all-gather.1
  114.5 40.6 all-reduce.1
  183.5 122.1 reduce-scatter.1
where the time goes:
time: 317 us
  waiting for transfers between devices  196 us (62%)
  matrix products  57 us (18%)
  starting transfers between devices  16.1 us (5%)
  between operations  14.6 us (5%)
  blocking collectives  12.2 us (4%)
  local copies, waits for them, and re-layouts  10.7 us (3%)
  other arithmetic  9.67 us (3%)
    reduce_scatter x1, waiting for transfers between devices, shards(): lax.psum_scatter((lax.dot_general(columns, delta_rows, (((0,), (0,)), (()...  122 us
    psum x1, waiting for transfers between devices, shards(): lax.psum(jnp.dot(activation, readout, preferred_element_type=jnp.float32)...  40.5 us
    dot_general x1, matrix products, shards(): lax.dot_general(columns, delta_rows, (((0,), (0,)), ((), ())), preferred_...  27.2 us
    all_gather x1, waiting for transfers between devices, shards(): lax.all_gather(weight, 'dp', axis=0, tiled=True)  19 us
    dot_general x1, matrix products, shards(): jnp.dot(columns, lax.all_gather(weight, 'dp', axis=0, tiled=True), prefer...  18.6 us
    all_gather x1, blocking collectives, shards(): lax.all_gather(block_patches, 'mp', axis=0, tiled=True)  12.2 us
    all_to_all x1, starting transfers between devices, shards(): lax.all_to_all(slot_marks, ('dp', 'mp'), split_axis=0, concat_axis=0, til...  11.1 us
    dot_general x1, matrix products, shards(): jnp.dot(lax.all_gather(block_patches, 'mp', axis=0, tiled=True), embed, p...  8.99 us
  transfers between devices with their start and end apart: 5, of which 5 were waited for; matrix products, arithmetic and copies ran while one was open for 6% of the time, Pallas kernels for 0%

commit v1 on v0

--- a/solution.py
+++ b/solution.py
@@ -10,6 +10,11 @@
 decay_rate = 0.1
 adam_epsilon = 1e-08
 step_count = 20
+
+
+def gather_over(array, mesh_axis, dim):
+    sent = jnp.stack([array] * lax.axis_size(mesh_axis))
+    return jnp.concatenate(lax.all_to_all(sent, mesh_axis, 0, 0), axis=dim)
 
 
 def gelu_tanh(value):
@@ -90,11 +95,7 @@
     width_scale = 1.0 / width**0.5
     columns = normed
     preact = (
-        jnp.dot(
-            columns,
-            lax.all_gather(weight, "dp", axis=0, tiled=True),
-            preferred_element_type=jnp.float32,
-        )
+        jnp.dot(columns, gather_over(weight, "dp", 0), preferred_element_type=jnp.float32)
         * width_scale
     )
     activation = gelu_tanh(preact).astype(jnp.bfloat16)

time: 317 us -> 522 us (1.65)
  waiting for transfers between devices: 196 us -> 390 us
  local copies, waits for them, and re-layouts: 10.7 us -> 17.4 us
  starting transfers between devices: 16.1 us -> 21.4 us
    all_to_all x0 -> x1, waiting for transfers between devices: none -> 217 us  [gather_over(): return jnp.concatenate(lax.all_to_all(sent, mesh_axis, 0, 0), axis=dim)]
    all_gather x1 -> x0, waiting for transfers between devices: 19 us -> none  [shards(): lax.all_gather(weight, 'dp', axis=0, tiled=True)]
    another operation x2 -> x3, local copies, waits for them, and re-layouts: 0.02 us -> 6.78 us  [the longest x1 6.76 us: gather_over(): sent = jnp.stack([array] * lax.axis_size(mesh_axis))]
    all_to_all x0 -> x1, starting transfers between devices: none -> 5.32 us  [gather_over(): return jnp.concatenate(lax.all_to_all(sent, mesh_axis, 0, 0), axis=dim)]
  transfers between devices with their start and end apart: 5 -> 5, of which waited for: 5 -> 5; matrix products, arithmetic and copies ran while one was open for 6% -> 3% of each run, Pallas kernels for 0% -> 0%
where the time goes in v1:
time: 522 us; the launch traced here: 521 us
  waiting for transfers between devices  390 us (75%)
  matrix products  56.9 us (11%)
  starting transfers between devices  21.4 us (4%)
  local copies, waits for them, and re-layouts  17.4 us (3%)
  between operations  15 us (3%)
  blocking collectives  12.2 us (2%)
  other arithmetic  8.74 us (2%)
    all_to_all x1, waiting for transfers between devices, gather_over(): return jnp.concatenate(lax.all_to_all(sent, mesh_axis, 0, 0), axis=dim)  217 us
    reduce_scatter x1, waiting for transfers between devices, shards(): lax.psum_scatter((lax.dot_general(columns, delta_rows, (((0,), (0,)), (()...  122 us
    psum x1, waiting for transfers between devices, shards(): lax.psum(jnp.dot(activation, readout, preferred_element_type=jnp.float32)...  35.7 us
    dot_general x1, matrix products, shards(): lax.dot_general(columns, delta_rows, (((0,), (0,)), ((), ())), preferred_...  27.2 us
    dot_general x1, matrix products, shards(): jnp.dot(columns, gather_over(weight, 'dp', 0), preferred_element_type=jnp...  18.6 us
    all_gather x1, blocking collectives, shards(): lax.all_gather(block_patches, 'mp', axis=0, tiled=True)  12.2 us
    all_to_all x1, starting transfers between devices, shards(): lax.all_to_all(slot_marks, ('dp', 'mp'), split_axis=0, concat_axis=0, til...  11.1 us
  transfers between devices with their start and end apart: 5, of which 5 were waited for; matrix products, arithmetic and copies ran while one was open for 3% of the time, Pallas kernels for 0%

profile of v1, /device:TPU:0, one launch (start us, length us, event | category | flops | bytes accessed | tf_op | source)
XLA Modules:
  0.0 521.2 jit_solution(5257630879746812408)
XLA Ops:
  7.2 0.0 copy-start
  7.9 0.7 add_select_fusion
  8.7 0.1 copy.18
  8.8 0.2 fusion.14
  9.0 0.1 broadcast_add_fusion
  9.1 0.2 fusion.16
  9.3 2.9 scatter_custom_fusion
  12.3 0.8 all_to_all.19
  13.1 11.1 %all-to-all-start = ((s32[128,3,1]{1,2,0:T(1,128)}), s32[128,3,1]{1,2,0:T(1,128)S(1)}, u32[]{:S(2)}, u32[]{:S(2)}) async-start(s32[128,3,1]{1,2,0:T(1,128)} %bitcast.5), calls=%async_computation | async-start | bytes 131072 | tf_op jit(solution)/shard_map/all_to_all | solution.py:76
  24.3 1.8 scatter_custom_fusion.1
  26.1 0.7 all_to_all.22
  26.8 6.7 %all-to-all-done = s32[128,3,1]{1,2,0:T(1,128)S(1)} async-done(((s32[128,3,1]{1,2,0:T(1,128)}), s32[128,3,1]{1,2,0:T(1,128)S(1)}, u32[]{:S(2)}, u32[]{:S(2)}) %all-to-all-start) | async-done | bytes 1568 | tf_op jit(solution)/shard_map/all_to_all | solution.py:76
  33.5 4.6 all-to-all-start.1
  38.1 1.3 convert_element_type.44
  39.5 8.1 %all-to-all-done.1 = bf16[128,3,128]{2,1,0:T(4,128)(2,1)S(1)} async-done(((bf16[128,3,128]{2,1,0:T(4,128)(2,1)}), bf16[128,3,128]{2,1,0:T(4,128)(2,1)S(1)}, u32[]{:S(2)}, u32[]{:S(2)}) %all-to-all-start.1) | async-done | bytes 98336 | tf_op jit(solution)/shard_map/all_to_all | solution.py:75
  47.6 6.8 %stack.2 = bf16[32,192,1536]{2,1,0:T(8,128)(2,1)} broadcast(bf16[192,1536]{1,0:T(8,128)(2,1)S(1)} %convert_element_type.44), dimensions={1,2} | broadcast | bytes 19464192 | tf_op jit(solution)/shard_map/stack | solution.py:16
  54.4 0.0 copy-start.4
  54.4 5.3 %all-to-all-start.2 = ((bf16[32,192,1536]{2,1,0:T(8,128)(2,1)}), bf16[32,192,1536]{2,1,0:T(8,128)(2,1)}, u32[]{:S(2)}, u32[]{:S(2)}) async-start(bf16[32,192,1536]{2,1,0:T(8,128)(2,1)} %stack.2), calls=%async_computation.2 | async-start | bytes 37748736 | tf_op jit(solution)/shard_map/all_to_all | solution.py:17
  59.7 0.0 all-reduce.2.cloned.1.call-start
  59.8 0.0 copy-done.4
  59.8 0.5 broadcast.115
  60.3 0.8 reduce.5
  61.1 0.2 all_to_all.21
  61.3 0.1 reshape.94
  61.4 1.4 scatter_custom_fusion.2
  62.9 12.2 %all_gather.3 = bf16[640,128]{1,0:T(8,128)(2,1)S(1)} all-gather(bf16[160,128]{1,0:T(8,128)(2,1)S(1)} %scatter_custom_fusion.2), channel_id=1, replica_groups=mesh['dp'=32,'mp'=4] {'mp'}, dimensions={0}, use_global_device_ids=true | all-gather | bytes 204800 | tf_op jit(solution)/shard_map/all_gather | solution.py:86
  75.1 0.0 copy-done
  75.1 8.9 %multiply_reduce_fusion = (f32[640]{0:T(1024)S(1)}, f32[640,6144]{1,0:T(8,128)}) fusion(bf16[640,128]{1,0:T(8,128)(2,1)S(1)} %all_gather.3, bf16[128,6144]{1,0:T(8,128)(2,1)S(1)} %copy-done), kind=kOutput, calls=%fused_computation.10 | convolution fusion | flops 1045953920 | bytes 17467904 | tf_op jit(solution)/shard_map/dot_general | solution.py:85
  84.0 216.7 %all-to-all-done.2 = bf16[32,192,1536]{2,1,0:T(8,128)(2,1)} async-done(((bf16[32,192,1536]{2,1,0:T(8,128)(2,1)}), bf16[32,192,1536]{2,1,0:T(8,128)(2,1)}, u32[]{:S(2)}, u32[]{:S(2)}) %all-to-all-start.2) | async-done | bytes 18874400 | tf_op jit(solution)/shard_map/all_to_all | solution.py:17
  300.7 18.6 %fusion.40 = f32[640,1536]{1,0:T(8,128)S(1)} fusion(bf16[6144,1536]{1,0:T(8,128)(2,1)} %bitcast.6, f32[640,6144]{1,0:T(8,128)} %get-tuple-element.12, f32[6144]{0:T(1024)S(1)} %convert_element_type.42, f32[640]{0:T(1024)S(1)} %add_rsqrt_fusion), kind=kOutput, calls=%fused_computation.67 | convolution fusion | flops 12091392000 | bytes 38562304 | tf_op jit(solution)/shard_map/dot_general | solution.py:98
  319.3 0.0 copy-start.7
  319.3 1.9 copy-done.7
  321.3 0.0 copy-done.5
  321.3 2.2 fusion.13
  323.4 0.0 all-reduce.2.cloned.1.call-update
  323.4 0.3 reduce-scatter.2.cloned.1.call-start
  323.7 35.7 %all-reduce.2.cloned.1.call-done = bf16[640,128]{1,0:T(8,128)(2,1)} async-done(((bf16[640,128]{1,0:T(8,128)(2,1)}), bf16[640,128]{1,0:T(8,128)(2,1)}) %all-reduce.2.cloned.1.call-update) | async-done | bytes 163856 | tf_op jit(solution)/shard_map/psum | solution.py:102
  359.4 0.9 convert_element_type.47
  360.3 0.0 copy-done.6
  360.3 0.0 copy-start.3
  360.3 27.2 %multiply_convert_fusion = bf16[6144,1536]{1,0:T(8,128)(2,1)} fusion(f32[640,1536]{1,0:T(8,128)} %copy-done.7, bf16[1536,128]{1,0:T(8,128)(2,1)S(1)} %copy-done.5, f32[640,128]{1,0:T(8,128)S(1)} %convert_element_type.47, bf16[640,128]{1,0:T(8,128)(2,1)S(1)} %copy-done.6, f32[640,6144]{1,0:T(8,128)} %get-tuple-element.12, f32[6144]{0:T(1024)S(1)} %convert_element_type.42, ...), kind=kOutput, calls=%fused_computation.3 | convolution fusion | flops 12381831168 | bytes 39447040 | tf_op jit(solution)/shard_map/dot_general | solution.py:113
  387.6 0.0 copy-done.3
  387.6 0.0 reduce-scatter.2.cloned.1.call-update
  387.6 0.0 copy-start.1
  387.6 122.3 %reduce-scatter.2.cloned.1.call-done = bf16[192,1536]{1,0:T(8,128)(2,1)} async-done(((bf16[6144,1536]{1,0:T(8,128)(2,1)}), bf16[192,1536]{1,0:T(8,128)(2,1)}) %reduce-scatter.2.cloned.1.call-update) | async-done | bytes 589840 | tf_op jit(solution)/shard_map/reduce_scatter | solution.py:111
  509.9 0.0 copy-done.2
  509.9 4.4 fusion.41
  514.3 0.0 copy-done.1
  (10 shorter events, 0.1 us)
Async XLA Ops:
  7.2 67.9 %copy-start = (bf16[128,6144]{1,0:T(8,128)(2,1)S(1)}, bf16[128,6144]{1,0:T(8,128)(2,1)}, u32[]{:S(2)}) copy-start(bf16[128,6144]{1,0:T(8,128)(2,1)} %param.15) | copy-start | bytes 4718596
  13.1 20.4 %all-to-all-start = ((s32[128,3,1]{1,2,0:T(1,128)}), s32[128,3,1]{1,2,0:T(1,128)S(1)}, u32[]{:S(2)}, u32[]{:S(2)}) async-start(s32[128,3,1]{1,2,0:T(1,128)} %bitcast.5), calls=%async_computation | async-start | bytes 131072 | tf_op jit(solution)/shard_map/all_to_all | solution.py:76
  33.5 14.1 %all-to-all-start.1 = ((bf16[128,3,128]{2,1,0:T(4,128)(2,1)}), bf16[128,3,128]{2,1,0:T(4,128)(2,1)S(1)}, u32[]{:S(2)}, u32[]{:S(2)}) async-start(bf16[128,3,128]{2,1,0:T(4,128)(2,1)} %all_to_all.22), calls=%async_computation.1 | async-start | bytes 262144 | tf_op jit(solution)/shard_map/all_to_all | solution.py:75
  54.4 5.4 %copy-start.4 = (bf16[6144]{0:T(1024)(128)(2,1)S(1)}, bf16[6144]{0:T(1024)(128)(2,1)}, u32[]{:S(2)}) copy-start(bf16[6144]{0:T(1024)(128)(2,1)} %param.16) | copy-start | bytes 36868
  54.4 246.3 %all-to-all-start.2 = ((bf16[32,192,1536]{2,1,0:T(8,128)(2,1)}), bf16[32,192,1536]{2,1,0:T(8,128)(2,1)}, u32[]{:S(2)}, u32[]{:S(2)}) async-start(bf16[32,192,1536]{2,1,0:T(8,128)(2,1)} %stack.2), calls=%async_computation.2 | async-start | bytes 37748736 | tf_op jit(solution)/shard_map/all_to_all | solution.py:17
  59.7 299.7 %all-reduce.2.cloned.1.call-start = ((), (), s32[]{:S(2)}) async-start(), calls=%async_computation.4 | async-start | bytes 327680 | tf_op jit(solution)/shard_map/psum | solution.py:102
  300.7 20.5 %copy-start.5 = (bf16[1536,128]{1,0:T(8,128)(2,1)S(1)}, bf16[1536,128]{1,0:T(8,128)(2,1)}, u32[]{:S(2)}) copy-start(bf16[1536,128]{1,0:T(8,128)(2,1)} %param.17) | copy-start | bytes 1179652
  319.3 1.9 copy-start.7
  321.3 39.1 %copy-start.6 = (bf16[640,128]{1,0:T(8,128)(2,1)S(1)}, bf16[640,128]{1,0:T(8,128)(2,1)}, u32[]{:S(2)}) copy-start(bf16[640,128]{1,0:T(8,128)(2,1)} %param.18) | copy-start | bytes 491524
  323.4 186.5 %reduce-scatter.2.cloned.1.call-start = ((), (), s32[]{:S(2)}) async-start(), calls=%async_computation.5 | async-start | bytes 19464192 | tf_op jit(solution)/shard_map/reduce_scatter | solution.py:111
  360.3 27.2 %copy-start.3 = (f32[640,128]{1,0:T(8,128)}, f32[640,128]{1,0:T(8,128)S(1)}, u32[]{:S(2)}) copy-start(f32[640,128]{1,0:T(8,128)S(1)} %convert_element_type.47) | copy-start | bytes 983044
  387.6 122.4 %copy-start.2 = (f32[192,1536]{1,0:T(8,128)S(1)}, f32[192,1536]{1,0:T(8,128)}, u32[]{:S(2)}) copy-start(f32[192,1536]{1,0:T(8,128)} %param.19) | copy-start | bytes 3538948
  387.6 126.8 %copy-start.1 = (bf16[128,6144]{1,0:T(8,128)(2,1)S(1)}, bf16[128,6144]{1,0:T(8,128)(2,1)}, u32[]{:S(2)}) copy-start(bf16[128,6144]{1,0:T(8,128)(2,1)} %param.15) | copy-start | bytes 4718596
Sparse Core Ops, SparseCore 0:
  323.6 35.7 all-reduce.1
  387.7 122.1 reduce-scatter.1
